TPU v7x, 512 devices: a whole 4x4x16 slice. The times are simulated.
512 devices in a mesh: dom: 128 (over x, z, core), tile: 4 (over y).
Axes of the slice: x: 4, y: 4, z: 16, core: 2. Of those that a mesh axis runs over, the one named last changes fastest.
Arguments:
- pumping: float32 [8192, 4096], P(('dom', 'tile')), may hold values from -36 to 36
- coupling: float32 [8192, 4096], P(('dom', 'tile')), may hold values from -0.75 to 0.75
- storage: float32 [8192, 64], P(('dom', 'tile')), may hold values from 0.2 to 2
- tile_order: int32 [512, 1024], P(('dom', 'tile')), may hold values from 0 to 1023, each once within a row
- kriging: bfloat16 [8192, 1024], P(('dom', 'tile')), may hold values from -0.75 to 0.75
Outputs:
- sensitivity: float32 [8192, 64], P(('dom', 'tile'))
- residual_gram: float32 [64, 64], replicated
All inputs are finite; a program needn't handle non-finite values.
Results may differ from a plain program's by a relative error of at most 0.00105.
Values may be sent and summed in bfloat16 or wider, within the bound.
No kernel may reach another device: no remote copies, remote signals or barrier semaphores. Data moves between devices by JAX's collectives and lax.ppermute only.
A program may use at most 64 MiB of HBM per device.

v0:
```python
import jax
import jax.numpy as jnp
from jax import lax
from jax.sharding import PartitionSpec as P

FX = 8
FY = 2
ITERS = 2
PRECISE = lax.Precision.HIGHEST


def padded_2(shard, sides, width):
    for axis, dim in sides:
        devices, length = (lax.axis_size(axis), shard.shape[dim])
        up = [(i, (i + 1) % devices) for i in range(devices - 1)]
        down = [(j, i) for i, j in up]
        last = lax.slice_in_dim(shard, length - width, length, axis=dim)
        initial = lax.slice_in_dim(shard, 0, width, axis=dim)
        before = lax.ppermute(last, axis, up)
        after = lax.ppermute(initial, axis, down)
        shard = jnp.concatenate([before, shard, after], axis=dim)
    return shard


def symmetric(matrix):
    return 0.5 * (matrix + matrix.T)


def gram_matrix(left, right):
    return jnp.einsum("brc,bsc->rs", left, right, precision=PRECISE)


def mix_rows(weights, values):
    return jnp.einsum("rs,brc->bsc", weights, values, precision=PRECISE)


def solve_definite(matrix, target):
    factor = jnp.linalg.cholesky(matrix)
    lower_part = lax.linalg.triangular_solve(factor, target, left_side=True, lower=True)
    return lax.linalg.triangular_solve(
        factor, lower_part, left_side=True, lower=True, transpose_a=True
    )


def total_squares(residual):
    return symmetric(lax.psum(gram_matrix(residual, residual), ("dom", "tile")))


def apply_operator(values, matrices, capacity):
    spread = jnp.einsum("brc,bce->bre", values, matrices, precision=PRECISE)
    patch_grid = spread.reshape(FX, FY, -1)
    padded = padded_2(patch_grid.astype(jnp.bfloat16), (("dom", 0), ("tile", 1)), 1).astype(
        patch_grid.dtype
    )
    beside = padded[:-2, 1:-1] + padded[2:, 1:-1] + padded[1:-1, :-2] + padded[1:-1, 2:]
    pulled = (4.0 * patch_grid - beside).reshape(values.shape)
    return capacity[:, None, :] * values + jnp.einsum(
        "bre,bce->brc", pulled, matrices, precision=PRECISE
    )


def shards(pumping, coupling, storage, tile_order, kriging):
    blocks = storage.shape[0]
    width_block = storage.shape[1]
    test_count = pumping.shape[1] // width_block
    groups = lax.axis_size("dom")
    matrices = coupling.reshape(blocks, width_block, width_block)
    residual = pumping.reshape(blocks, test_count, width_block)
    direction = residual
    solution = jnp.zeros_like(residual)
    residual_gram = total_squares(residual)
    for iteration in range(ITERS):
        applied = apply_operator(direction, matrices, storage)
        curvature = symmetric(lax.psum(gram_matrix(direction, applied), ("dom", "tile")))
        step_size = solve_definite(curvature, residual_gram)
        solution = solution + mix_rows(step_size, direction)
        residual = residual - mix_rows(step_size, applied)
        next_gram = total_squares(residual)
        if iteration + 1 < ITERS:
            direction = residual + mix_rows(solve_definite(residual_gram, next_gram), direction)
        residual_gram = next_gram
    head_table = jnp.transpose(solution, (1, 0, 2)).reshape(test_count, -1)
    ordered = jnp.take(head_table, tile_order[0], axis=1).reshape(test_count, groups, -1)
    arrived = lax.all_to_all(ordered, "dom", split_axis=1, concat_axis=1, tiled=True).reshape(
        test_count, -1
    )
    sensitivity = lax.dot_general(
        kriging.astype(jnp.float32), arrived, (((1,), (1,)), ((), ())), precision=PRECISE
    )
    cell_total = blocks * width_block * groups * lax.axis_size("tile")
    return (sensitivity, residual_gram / cell_total)


def solution(mesh):
    in_specs = (
        P(("dom", "tile"), None),
        P(("dom", "tile"), None),
        P(("dom", "tile"), None),
        P(("dom", "tile"), None),
        P(("dom", "tile"), None),
    )
    out_specs = (P(("dom", "tile"), None), P())
    return jax.shard_map(shards, mesh=mesh, in_specs=in_specs, out_specs=out_specs, check_vma=False)
```

profile of v0, /device:TPU:1, one launch (start us, length us, event | category | flops | bytes accessed | tf_op | source)
XLA Modules:
  0.0 525.7 jit_solution(12580467156202745954)
XLA Ops:
  2.9 4.9 collective-permute-start
  7.9 5.1 collective-permute-start.1
  15.3 1.3 collective-permute-start.3
  16.6 4.0 collective-permute-start.2
  21.2 1.9 collective-permute-done.3
  23.1 1.4 collective-permute-done.2
  27.6 109.2 %all-reduce = (f32[64,64]{1,0:T(8,128)S(1)}, f32[64,64]{1,0:T(8,128)S(1)}) all-reduce(f32[64,64]{1,0:T(8,128)S(1)} %convolution_bitcast_fusion.9, f32[64,64]{1,0:T(8,128)S(1)} %convolution_bitcast_fusion.10), channel_id=1, replica_groups=mesh['dom'=128,'tile'=4] {'dom','tile'}, use_global_device_ids=true, to_apply=%region_3.0 | all-reduce | flops 8192 | bytes 65536 | tf_op jit(solution)/shard_map/psum | solution.py:46
  137.0 5.8 %cholesky.59 = f32[64,64]{1,0:T(8,128)S(1)} custom-call(f32[64,64]{1,0:T(8,128)S(1)} %fusion.24), custom_call_target="Cholesky" | custom-call | tf_op jit(solution)/shard_map/jit(cholesky)/cholesky | solution.py:38
  144.2 4.9 custom-call.13
  150.3 5.8 %cholesky.70 = f32[64,64]{1,0:T(8,128)S(1)} custom-call(f32[64,64]{1,0:T(8,128)S(1)} %fusion.19), custom_call_target="Cholesky" | custom-call | tf_op jit(solution)/shard_map/jit(cholesky)/cholesky | solution.py:38
  157.5 4.9 custom-call.15
  162.9 99.0 %psum.37 = f32[64,64]{1,0:T(8,128)S(1)} all-reduce(f32[64,64]{1,0:T(8,128)S(1)} %convolution_bitcast_fusion.7), channel_id=1, replica_groups=mesh['dom'=128,'tile'=4] {'dom','tile'}, use_global_device_ids=true, to_apply=%region_4.8 | all-reduce | flops 4096 | bytes 32768 | tf_op jit(solution)/shard_map/psum | solution.py:46
  263.8 4.2 collective-permute-start.4
  268.4 1.9 collective-permute-start.5
  270.5 3.0 collective-permute-done.5
  275.9 4.7 collective-permute-start.6
  281.4 1.5 collective-permute-done.6
  282.9 1.5 maximum_convert_fusion.1
  286.7 101.5 %psum.38 = f32[64,64]{1,0:T(8,128)S(1)} all-reduce(f32[64,64]{1,0:T(8,128)S(1)} %convolution_bitcast_fusion.5), channel_id=1, replica_groups=mesh['dom'=128,'tile'=4] {'dom','tile'}, use_global_device_ids=true, to_apply=%region_5.9 | all-reduce | flops 4096 | bytes 32768 | tf_op jit(solution)/shard_map/psum | solution.py:74
  388.4 5.8 %cholesky.81 = f32[64,64]{1,0:T(8,128)S(1)} custom-call(f32[64,64]{1,0:T(8,128)S(1)} %fusion.13), custom_call_target="Cholesky" | custom-call | tf_op jit(solution)/shard_map/jit(cholesky)/cholesky | solution.py:38
  395.6 4.9 custom-call.17
  401.7 2.8 gather_fusion
  405.8 10.6 %all-to-all-start = ((f32[128,1,512]{2,1,0:T(1,128)}), f32[128,1,512]{2,1,0:T(1,128)S(1)}, u32[]{:S(2)}, u32[]{:S(2)}) async-start(f32[128,1,512]{2,1,0:T(1,128)} %reshape.146), calls=%async_computation | async-start | bytes 524288 | tf_op jit(solution)/shard_map/all_to_all | solution.py:84
  417.6 104.6 %psum.39 = f32[64,64]{1,0:T(8,128)S(1)} all-reduce(f32[64,64]{1,0:T(8,128)S(1)} %convolution_bitcast_fusion.3), channel_id=1, replica_groups=mesh['dom'=128,'tile'=4] {'dom','tile'}, use_global_device_ids=true, to_apply=%region_6.10 | all-reduce | flops 4096 | bytes 32768 | tf_op jit(solution)/shard_map/psum | solution.py:46
  (95 shorter events, 29.0 us)
Async XLA Ops:
  0.6 524.2 %copy-start = (bf16[16,1024]{1,0:T(8,128)(2,1)S(1)}, bf16[16,1024]{1,0:T(8,128)(2,1)}, u32[]{:S(2)}) copy-start(bf16[16,1024]{1,0:T(8,128)(2,1)} %param.14) | copy-start | bytes 98308
  0.6 1.2 copy-start.1
  2.9 12.0 %collective-permute-start = (bf16[1,2,4096]{2,1,0:T(2,128)(2,1)S(1)}, bf16[1,2,4096]{2,1,0:T(2,128)(2,1)S(1)}, u32[]{:S(2)}, u32[]{:S(2)}) collective-permute-start(bf16[1,2,4096]{2,1,0:T(2,128)(2,1)S(1)} %slice.69), channel_id=1, source_target_pairs={{0,4},{4,8},{8,12},{12,16},{16,20},{20,24},{24,28},{28,32},{32,36}... | collective-permute-start | bytes 49160 | tf_op jit(solution)/shard_map/ppermute | solution.py:19
  7.8 5.8 %copy-start.3 = (s32[1,1024]{1,0:T(1,128)S(1)}, s32[1,1024]{1,0:T(1,128)}, u32[]{:S(2)}) copy-start(s32[1,1024]{1,0:T(1,128)} %param.13) | copy-start | bytes 12292
  7.9 7.1 %collective-permute-start.1 = (bf16[1,2,4096]{2,1,0:T(2,128)(2,1)S(1)}, bf16[1,2,4096]{2,1,0:T(2,128)(2,1)S(1)}, u32[]{:S(2)}, u32[]{:S(2)}) collective-permute-start(bf16[1,2,4096]{2,1,0:T(2,128)(2,1)S(1)} %slice.71), channel_id=1, source_target_pairs={{4,0},{8,4},{12,8},{16,12},{20,16},{24,20},{28,24},{32,28},{36,32}... | collective-permute-start | bytes 49160 | tf_op jit(solution)/shard_map/ppermute | solution.py:20
  15.3 7.8 %collective-permute-start.3 = (bf16[10,1,4096]{2,1,0:T(2,128)(2,1)S(1)}, bf16[10,1,4096]{2,1,0:T(2,128)(2,1)S(1)}, u32[]{:S(2)}, u32[]{:S(2)}) collective-permute-start(bf16[10,1,4096]{2,1,0:T(2,128)(2,1)S(1)} %get-tuple-element.18), channel_id=1, source_target_pairs={{1,0},{2,1},{3,2},{5,4},{6,5},{7,6},{9,8},{10,9},{11,10},{13,12},{... | collective-permute-start | bytes 245768 | tf_op jit(solution)/shard_map/ppermute | solution.py:20
  16.6 7.9 %collective-permute-start.2 = (bf16[10,1,4096]{2,1,0:T(2,128)(2,1)S(1)}, bf16[10,1,4096]{2,1,0:T(2,128)(2,1)S(1)}, u32[]{:S(2)}, u32[]{:S(2)}) collective-permute-start(bf16[10,1,4096]{2,1,0:T(2,128)(2,1)S(1)} %get-tuple-element.17), channel_id=1, source_target_pairs={{0,1},{1,2},{2,3},{4,5},{5,6},{6,7},{8,9},{9,10},{10,11},{12,13},{... | collective-permute-start | bytes 245768 | tf_op jit(solution)/shard_map/ppermute | solution.py:19
  25.3 0.7 copy-start.2
  263.8 6.5 %collective-permute-start.4 = (bf16[1,2,4096]{2,1,0:T(2,128)(2,1)S(1)}, bf16[1,2,4096]{2,1,0:T(2,128)(2,1)S(1)}, u32[]{:S(2)}, u32[]{:S(2)}) collective-permute-start(bf16[1,2,4096]{2,1,0:T(2,128)(2,1)S(1)} %slice.79), channel_id=1, source_target_pairs={{0,4},{4,8},{8,12},{12,16},{16,20},{20,24},{24,28},{28,32},{32,36}... | collective-permute-start | bytes 49160 | tf_op jit(solution)/shard_map/ppermute | solution.py:19
  268.4 5.1 collective-permute-start.5
  274.6 6.8 %collective-permute-start.7 = (bf16[10,1,4096]{2,1,0:T(2,128)(2,1)}, bf16[10,1,4096]{2,1,0:T(2,128)(2,1)}, u32[]{:S(2)}, u32[]{:S(2)}) collective-permute-start(bf16[10,1,4096]{2,1,0:T(2,128)(2,1)} %get-tuple-element.16), channel_id=1, source_target_pairs={{1,0},{2,1},{3,2},{5,4},{6,5},{7,6},{9,8},{10,9},{11,10},{13,12},{... | collective-permute-start | bytes 245768 | tf_op jit(solution)/shard_map/ppermute | solution.py:20
  275.9 7.1 %collective-permute-start.6 = (bf16[10,1,4096]{2,1,0:T(2,128)(2,1)}, bf16[10,1,4096]{2,1,0:T(2,128)(2,1)}, u32[]{:S(2)}, u32[]{:S(2)}) collective-permute-start(bf16[10,1,4096]{2,1,0:T(2,128)(2,1)} %get-tuple-element.15), channel_id=1, source_target_pairs={{0,1},{1,2},{2,3},{4,5},{5,6},{6,7},{8,9},{9,10},{10,11},{12,13},{... | collective-permute-start | bytes 245768 | tf_op jit(solution)/shard_map/ppermute | solution.py:19
  405.8 117.1 %all-to-all-start = ((f32[128,1,512]{2,1,0:T(1,128)}), f32[128,1,512]{2,1,0:T(1,128)S(1)}, u32[]{:S(2)}, u32[]{:S(2)}) async-start(f32[128,1,512]{2,1,0:T(1,128)} %reshape.146), calls=%async_computation | async-start | bytes 524288 | tf_op jit(solution)/shard_map/all_to_all | solution.py:84
where the time goes:
time: 527 us; the launch traced here: 526 us
  blocking collectives  414 us (79%)
  other arithmetic  41.7 us (8%)
  starting transfers between devices  38.1 us (7%)
  local copies, waits for them, and re-layouts  11.3 us (2%)
  matrix products  11.3 us (2%)
  waiting for transfers between devices  7.81 us (1%)
    psum x3, blocking collectives, total_squares(): return symmetric(lax.psum(gram_matrix(residual, residual), ('dom', 'tile')))  313 us
    psum x1, blocking collectives, shards(): lax.psum(gram_matrix(direction, applied), ('dom', 'tile'))  102 us
    another operation x9, other arithmetic, solve_definite(): factor = jnp.linalg.cholesky(matrix)  19.6 us
    ppermute x4, starting transfers between devices, padded_2(): before = lax.ppermute(last, axis, up)  17.8 us
    another operation x6, other arithmetic, solve_definite(): lax.linalg.triangular_solve(factor, lower_part, left_side=True, lower=Tru...  16.6 us
    all_to_all x1, starting transfers between devices, shards(): lax.all_to_all(ordered, 'dom', split_axis=1, concat_axis=1, tiled=True)  10.6 us
  transfers between devices with their start and end apart: 9, of which 4 were waited for; matrix products, arithmetic and copies ran while one was open for 1% of the time, Pallas kernels for 0%

commit v1 on v0

--- a/solution.py
+++ b/solution.py
@@ -43,7 +43,9 @@
 
 
 def total_squares(residual):
-    return symmetric(lax.psum(gram_matrix(residual, residual), ("dom", "tile")))
+    return symmetric(
+        jnp.sum(lax.all_gather(gram_matrix(residual, residual), ("dom", "tile")), axis=0)
+    )
 
 
 def apply_operator(values, matrices, capacity):

time: 527 us -> 841 us (1.60)
  waiting for transfers between devices: 7.81 us -> 470 us
  blocking collectives: 414 us -> 245 us
  other arithmetic: 41.7 us -> 62.4 us
  starting transfers between devices: 38.1 us -> 23.4 us
  between operations: 1.21 us -> 14.3 us
    all_gather x0 -> x3, waiting for transfers between devices: none -> 455 us  [total_squares(): lax.all_gather(gram_matrix(residual, residual), ('dom', 'tile'))]
    psum x3 -> x0, blocking collectives: 313 us -> none  [total_squares(): return symmetric(lax.psum(gram_matrix(residual, residual), ('dom', 'tile')))]
    psum x1 -> x2, blocking collectives: 102 us -> 212 us  [shards(): lax.psum(gram_matrix(direction, applied), ('dom', 'tile'))]
    all_to_all x0 -> x1, blocking collectives: none -> 33 us  [shards(): lax.all_to_all(ordered, 'dom', split_axis=1, concat_axis=1, tiled=True)]
    reduce_sum x0 -> x3, other arithmetic: none -> 20.8 us  [total_squares(): jnp.sum(lax.all_gather(gram_matrix(residual, residual), ('dom', 'tile')),...]
    all_to_all x1 -> x0, starting transfers between devices: 10.6 us -> none  [shards(): lax.all_to_all(ordered, 'dom', split_axis=1, concat_axis=1, tiled=True)]
  transfers between devices with their start and end apart: 9 -> 11, of which waited for: 4 -> 9; matrix products, arithmetic and copies ran while one was open for 1% -> 5% of each run, Pallas kernels for 0% -> 0%
where the time goes in v1:
time: 841 us; the launch traced here: 840 us
  waiting for transfers between devices  470 us (56%)
  blocking collectives  245 us (29%)
  other arithmetic  62.4 us (7%)
  starting transfers between devices  23.4 us (3%)
  between operations  14.3 us (2%)
  matrix products  13.9 us (2%)
  local copies, waits for them, and re-layouts  11.2 us (1%)
    all_gather x3, waiting for transfers between devices, total_squares(): lax.all_gather(gram_matrix(residual, residual), ('dom', 'tile'))  455 us
    psum x2, blocking collectives, shards(): lax.psum(gram_matrix(direction, applied), ('dom', 'tile'))  212 us
    all_to_all x1, blocking collectives, shards(): lax.all_to_all(ordered, 'dom', split_axis=1, concat_axis=1, tiled=True)  33 us
    reduce_sum x3, other arithmetic, total_squares(): jnp.sum(lax.all_gather(gram_matrix(residual, residual), ('dom', 'tile')),...  20.8 us
    another operation x9, other arithmetic, solve_definite(): factor = jnp.linalg.cholesky(matrix)  19.6 us
  transfers between devices with their start and end apart: 11, of which 9 were waited for; matrix products, arithmetic and copies ran while one was open for 5% of the time, Pallas kernels for 0%

profile of v1, /device:TPU:1, one launch (start us, length us, event | category | flops | bytes accessed | tf_op | source)
XLA Modules:
  0.0 840.0 jit_solution(985364512428779074)
XLA Ops:
  11.6 4.9 collective-permute-start
  16.6 5.1 collective-permute-start.1
  22.9 2.3 collective-permute-start.2
  28.7 4.2 collective-permute-done.3
  36.4 109.5 %psum.14 = f32[64,64]{1,0:T(8,128)S(1)} all-reduce(f32[64,64]{1,0:T(8,128)S(1)} %convolution_bitcast_fusion.10), channel_id=1, replica_groups=mesh['dom'=128,'tile'=4] {'dom','tile'}, use_global_device_ids=true, to_apply=%region_0.0 | all-reduce | flops 4096 | bytes 32768 | tf_op jit(solution)/shard_map/psum | solution.py:76
  146.1 5.8 cholesky.59
  153.3 4.9 custom-call.13
  158.2 80.4 %all-gather.7.cloned.1.call-done = f32[32768,64]{1,0:T(8,128)} async-done(((f32[64,64]{1,0:T(8,128)}), f32[32768,64]{1,0:T(8,128)}) %all-gather.7.cloned.1.call-update) | async-done | bytes 8388624 | tf_op jit(solution)/shard_map/all_gather | solution.py:47
  238.6 6.9 reduce_sum.27
  248.2 5.8 cholesky.70
  255.4 4.9 custom-call.15
  260.3 202.8 %all-gather.9.cloned.1.call-done = f32[32768,64]{1,0:T(8,128)} async-done(((f32[64,64]{1,0:T(8,128)}), f32[32768,64]{1,0:T(8,128)}) %all-gather.9.cloned.1.call-update) | async-done | bytes 8388624 | tf_op jit(solution)/shard_map/all_gather | solution.py:47
  463.1 6.9 reduce_sum.28
  472.0 3.3 collective-permute-start.4
  477.7 3.0 collective-permute-done.5
  481.8 2.9 collective-permute-start.6
  487.5 4.1 collective-permute-done.7
  495.3 102.2 %psum.15 = f32[64,64]{1,0:T(8,128)S(1)} all-reduce(f32[64,64]{1,0:T(8,128)S(1)} %convolution_bitcast_fusion.5), channel_id=1, replica_groups=mesh['dom'=128,'tile'=4] {'dom','tile'}, use_global_device_ids=true, to_apply=%region_5.9 | all-reduce | flops 4096 | bytes 32768 | tf_op jit(solution)/shard_map/psum | solution.py:76
  597.6 5.8 cholesky.81
  604.8 4.9 custom-call.17
  614.8 2.8 gather_fusion
  618.1 33.0 %all_to_all.5 = f32[128,1,512]{2,1,0:T(1,128)S(1)} all-to-all(f32[128,1,512]{2,1,0:T(1,128)S(1)} %reshape.149), channel_id=1, replica_groups=mesh['dom'=128,'tile'=4] {'dom'}, dimensions={0} | all-to-all | bytes 524288 | tf_op jit(solution)/shard_map/all_to_all | solution.py:86
  653.9 171.9 %all-gather.11.cloned.1.call-done = f32[32768,64]{1,0:T(8,128)} async-done(((f32[64,64]{1,0:T(8,128)}), f32[32768,64]{1,0:T(8,128)}) %all-gather.11.cloned.1.call-update) | async-done | bytes 8388624 | tf_op jit(solution)/shard_map/all_gather | solution.py:47
  825.8 6.9 reduce_sum.29
  (103 shorter events, 40.1 us)
Async XLA Ops:
  7.2 645.8 %copy-start = (bf16[16,1024]{1,0:T(8,128)(2,1)S(1)}, bf16[16,1024]{1,0:T(8,128)(2,1)}, u32[]{:S(2)}) copy-start(bf16[16,1024]{1,0:T(8,128)(2,1)} %param.14) | copy-start | bytes 98308
  7.2 231.4 %all-gather.7.cloned.1.call-start = ((), (), s32[]{:S(2)}) async-start(), calls=%async_computation.1 | async-start | bytes 16809984 | tf_op jit(solution)/shard_map/all_gather | solution.py:47
  9.6 453.6 %all-gather.9.cloned.1.call-start = ((), (), s32[]{:S(2)}) async-start(), calls=%async_computation.2 | async-start | bytes 16809984 | tf_op jit(solution)/shard_map/all_gather | solution.py:47
  11.6 10.4 %collective-permute-start = (bf16[1,2,4096]{2,1,0:T(2,128)(2,1)S(1)}, bf16[1,2,4096]{2,1,0:T(2,128)(2,1)S(1)}, u32[]{:S(2)}, u32[]{:S(2)}) collective-permute-start(bf16[1,2,4096]{2,1,0:T(2,128)(2,1)S(1)} %slice.69), channel_id=1, source_target_pairs={{0,4},{4,8},{8,12},{12,16},{16,20},{20,24},{24,28},{28,32},{32,36}... | collective-permute-start | bytes 49160 | tf_op jit(solution)/shard_map/ppermute | solution.py:19
  16.6 6.0 collective-permute-start.1
  22.9 5.8 collective-permute-start.2
  25.2 7.7 collective-permute-start.3
  245.5 248.2 %copy-start.1 = (f32[16,64]{1,0:T(8,128)S(1)}, f32[16,64]{1,0:T(8,128)}, u32[]{:S(2)}) copy-start(f32[16,64]{1,0:T(8,128)} %param.12) | copy-start | bytes 12292
  247.9 364.6 %copy-start.2 = (s32[1,1024]{1,0:T(1,128)S(1)}, s32[1,1024]{1,0:T(1,128)}, u32[]{:S(2)}) copy-start(s32[1,1024]{1,0:T(1,128)} %param.13) | copy-start | bytes 12292
  247.9 577.9 %all-gather.11.cloned.1.call-start = ((), (), s32[]{:S(2)}) async-start(), calls=%async_computation.3 | async-start | bytes 16809984 | tf_op jit(solution)/shard_map/all_gather | solution.py:47
  472.0 5.6 collective-permute-start.4
  475.7 5.1 collective-permute-start.5
  481.8 5.7 collective-permute-start.6
  484.7 6.9 collective-permute-start.7
Sparse Core Ops, SparseCore 0:
  13.0 225.5 all-gather.6
  248.0 215.1 all-gather.8
  612.1 213.6 all-gather.10
